TPU v7x, 128 devices: a whole 4x4x4 slice. The times are simulated.
128 devices in a mesh: ctx: 16 (over x_lo, z, core), tp: 8 (over y, x_hi).
Axes of the slice: x: 4 (x_hi: 2, x_lo: 2; x = x_hi * 2 + x_lo), y: 4, z: 4, core: 2. Of those that a mesh axis runs over, the one named last changes fastest.
Arguments:
- tokens: bfloat16 [16384, 1024], P(('ctx', 'tp')), may hold values from -6 to 6
- block_table: int32 [16, 2], replicated, may hold values from 0 to 31, as said below
- doc_ids: int32 [4, 4096], replicated, may hold values from 0 to 3, never falling along the last dimension, each value on 1 to 2048 neighbouring positions
- attn_gain: bfloat16 [1024], P('ctx'), may hold values from 0.25 to 1.75
- w_query: bfloat16 [1024, 2048], P('ctx', 'tp'), may hold values from -0.1875 to 0.1875
- w_key: bfloat16 [1024, 1024], P('ctx', 'tp'), may hold values from -0.1875 to 0.1875
- w_value: bfloat16 [1024, 1024], P('ctx', 'tp'), may hold values from -0.1875 to 0.1875
- query_gain: bfloat16 [128], P('ctx'), may hold values from 0.25 to 1.75
- key_gain: bfloat16 [128], P('ctx'), may hold values from 0.25 to 1.75
- w_out: bfloat16 [2048, 1024], P('tp', 'ctx'), may hold values from -1 to 1
- ffn_gain: bfloat16 [1024], P('ctx'), may hold values from 0.25 to 1.75
- w_gate: bfloat16 [1024, 3072], P('ctx', 'tp'), may hold values from -0.1875 to 0.1875
- w_up: bfloat16 [1024, 3072], P('ctx', 'tp'), may hold values from -0.1875 to 0.1875
- w_down: bfloat16 [3072, 1024], P('tp', 'ctx'), may hold values from -0.109375 to 0.109375
- out_grad: bfloat16 [16384, 1024], P(('ctx', 'tp')), may hold values from -6 to 6
Outputs:
- out: bfloat16 [16384, 1024], P(('ctx', 'tp'))
- grad_x: bfloat16 [16384, 1024], P(('ctx', 'tp'))
- grad_attn_gain: float32 [1024], P('ctx')
- grad_w_query: float32 [1024, 2048], P('ctx', 'tp')
- grad_w_key: float32 [1024, 1024], P('ctx', 'tp')
- grad_w_value: float32 [1024, 1024], P('ctx', 'tp')
- grad_query_gain: float32 [128], P('ctx')
- grad_key_gain: float32 [128], P('ctx')
- grad_w_out: float32 [2048, 1024], P('tp', 'ctx')
- grad_ffn_gain: float32 [1024], P('ctx')
- grad_w_gate: float32 [1024, 3072], P('ctx', 'tp')
- grad_w_up: float32 [1024, 3072], P('ctx', 'tp')
- grad_w_down: float32 [3072, 1024], P('tp', 'ctx')
Inputs may be any that keep to these rules, and one draw needn't show every extreme that they name: `block_table`: row c holds a block b below 16 and its mirror 2 * 16 - 1 - b; the first entries of the rows form a permutation, so every block appears once. `doc_ids`: never falling along a row; each document has 1 to 2048 positions, one exactly that many.
All inputs are finite; a program needn't handle non-finite values.
Results may differ from a plain program's by a relative error of at most 0.025.
Values may be sent and summed in bfloat16 or wider, within the bound.
No kernel may reach another device: no remote copies, remote signals or barrier semaphores. Data moves between devices by JAX's collectives and lax.ppermute only.
A program may use at most 192 MiB of HBM per device.

v0:
```python
import math
import jax
import jax.numpy as jnp
from jax import lax
from jax.sharding import PartitionSpec as P

HD = 128
EPS = 1e-06
THETA = 1000000.0
NEG_SCORE = -1e30


def split_up(shard, dim, length):
    before, after = (shard.shape[:dim], shard.shape[dim + 1 :])
    return jnp.moveaxis(shard.reshape(*before, length, -1, *after), dim, 0)


def sent_and_summed(shard, axis, dim):
    parts = split_up(shard, dim, lax.axis_size(axis))
    arrived = lax.all_to_all(parts, axis, split_axis=0, concat_axis=0, tiled=True)
    return arrived.astype(jnp.float32).sum(axis=0)


def normed(values, norm_gain):
    return values * lax.rsqrt(jnp.mean(values * values, axis=-1, keepdims=True) + EPS) * norm_gain


def rotate(values, cos_table, sin_table):
    half_width = values.shape[-1] // 2
    turned = jnp.concatenate([-values[..., half_width:], values[..., :half_width]], axis=-1)
    return values * cos_table + turned * sin_table


def contract_last(left_side, right_side):
    return lax.dot_general(
        left_side, right_side, (((1,), (1,)), ((), ())), preferred_element_type=jnp.float32
    )


def contract_first(left_side, right_side):
    return lax.dot_general(
        left_side, right_side, (((0,), (0,)), ((), ())), preferred_element_type=jnp.float32
    )


def send_grads(stacked):
    return lax.psum_scatter(
        stacked.astype(jnp.bfloat16), "ctx", scatter_dimension=0, tiled=True
    ).astype(jnp.float32)


def per_device(
    tokens,
    block_table,
    doc_ids,
    attn_gain,
    w_query,
    w_key,
    w_value,
    query_gain,
    key_gain,
    w_out,
    ffn_gain,
    w_gate,
    w_up,
    w_down,
    out_grad,
):
    ctx_count = lax.axis_size("ctx")
    tp_count = lax.axis_size("tp")
    ctx_rank = lax.axis_index("ctx")
    rows_dev = tokens.shape[0]
    local_rows = rows_dev * tp_count
    seq_count = doc_ids.shape[0]
    pair_rows = local_rows // seq_count
    seq_keys = pair_rows * ctx_count
    q_heads = w_query.shape[1] // HD
    kv_heads = w_key.shape[1] // HD
    group_size = q_heads // kv_heads
    q_width = q_heads * HD
    k_width = kv_heads * HD
    ff_local = w_gate.shape[1]
    score_scale = HD ** (-0.5)
    key_block = math.gcd(seq_keys, 512)
    key_blocks = seq_keys // key_block
    seq_len = doc_ids.shape[1]
    half_block = pair_rows // 2
    seq_index = jnp.arange(seq_len, dtype=jnp.int32)
    change = jnp.concatenate(
        [jnp.ones((seq_count, 1), dtype=bool), doc_ids[:, 1:] != doc_ids[:, :-1]], axis=1
    )
    doc_starts = lax.cummax(jnp.where(change, seq_index[None, :], 0), axis=1)
    key_index = jnp.arange(seq_keys, dtype=jnp.int32)
    key_inner = key_index % pair_rows
    key_place = (
        block_table[key_index // pair_rows, key_inner // half_block] * half_block
        + key_inner % half_block
    )
    key_doc = doc_ids[:, key_place]
    query_index = jnp.arange(local_rows, dtype=jnp.int32)
    query_seq = query_index // pair_rows
    query_inner = query_index % pair_rows
    query_place = (
        block_table[jnp.zeros_like(query_index) + ctx_rank, query_inner // half_block] * half_block
        + query_inner % half_block
    )
    query_doc = doc_ids[query_seq, query_place]
    query_pos = query_place - doc_starts[query_seq, query_place]
    query_place_s = query_place.reshape(seq_count, pair_rows)
    query_doc_s = query_doc.reshape(seq_count, pair_rows)
    freq_steps = jnp.arange(HD // 2, dtype=jnp.float32) * (2.0 / HD)
    angles = (
        query_pos.astype(jnp.float32)[:, None] * jnp.power(jnp.float32(THETA), -freq_steps)[None, :]
    )
    angles = jnp.concatenate([angles, angles], axis=1)[:, None, :]
    cos_table = jnp.cos(angles)
    sin_table = jnp.sin(angles)
    gain_attn, gain_query, gain_key, w_qkv, w_proj = (
        lax.all_gather(attn_gain, "ctx", axis=0, tiled=True),
        lax.all_gather(query_gain, "ctx", axis=0, tiled=True),
        lax.all_gather(key_gain, "ctx", axis=0, tiled=True),
        lax.all_gather(
            jnp.concatenate([w_query, w_key, w_value], axis=1), "ctx", axis=0, tiled=True
        ),
        lax.all_gather(w_out, "ctx", axis=1, tiled=True),
    )
    tokens_f = tokens.astype(jnp.float32)
    normal_one_f, norm_one_back = jax.vjp(normed, tokens_f, gain_attn.astype(jnp.float32))
    normal_one = normal_one_f.astype(jnp.bfloat16)
    rows_one = lax.all_gather(normal_one, "tp", axis=0, tiled=True)
    projected = jnp.dot(rows_one, w_qkv, preferred_element_type=jnp.float32)
    query_pre = projected[:, :q_width].reshape(local_rows, q_heads, HD)
    key_pre = projected[:, q_width : q_width + k_width].reshape(local_rows, kv_heads, HD)
    value_low = projected[:, q_width + k_width :].astype(jnp.bfloat16)

    def head_prep(pre_values, norm_gain):
        return rotate(normed(pre_values, norm_gain), cos_table, sin_table)

    query_rot, query_back = jax.vjp(head_prep, query_pre, gain_query.astype(jnp.float32))
    key_rot, key_back = jax.vjp(head_prep, key_pre, gain_key.astype(jnp.float32))
    query_low = query_rot.astype(jnp.bfloat16).reshape(
        seq_count, pair_rows, kv_heads, group_size, HD
    )
    key_low = key_rot.astype(jnp.bfloat16).reshape(seq_count, pair_rows, k_width)
    own_values = value_low.reshape(seq_count, pair_rows, k_width)
    keys_all, values_all = (
        lax.all_gather(key_low, "ctx", axis=1, tiled=True),
        lax.all_gather(own_values, "ctx", axis=1, tiled=True),
    )
    keys_seq = keys_all.reshape(seq_count, seq_keys, kv_heads, HD)
    values_seq = values_all.reshape(seq_count, seq_keys, kv_heads, HD)

    def tile_at(start):
        key_tile = lax.dynamic_slice_in_dim(keys_seq, start, key_block, 1)
        value_tile = lax.dynamic_slice_in_dim(values_seq, start, key_block, 1)
        place_tile = lax.dynamic_slice_in_dim(key_place, start, key_block, 0)
        doc_tile = lax.dynamic_slice_in_dim(key_doc, start, key_block, 1)
        scores = (
            jnp.einsum("sqhgd,skhd->shgqk", query_low, key_tile, preferred_element_type=jnp.float32)
            * score_scale
        )
        allowed = (doc_tile[:, None, :] == query_doc_s[:, :, None]) & (
            place_tile[None, None, :] <= query_place_s[:, :, None]
        )
        return (key_tile, value_tile, scores, allowed[:, None, None, :, :])

    starts = jnp.arange(key_blocks, dtype=jnp.int32) * key_block

    def stats_step(running, start):
        peak_score, row_total = running
        key_tile, value_tile, scores, allowed = tile_at(start)
        scores = jnp.where(allowed, scores, NEG_SCORE)
        new_peak = jnp.maximum(peak_score, jnp.max(scores, axis=-1))
        weights = jnp.where(allowed, jnp.exp(scores - new_peak[..., None]), 0.0)
        row_total = row_total * jnp.exp(peak_score - new_peak) + jnp.sum(weights, axis=-1)
        return ((new_peak, row_total), None)

    stat_shape = (seq_count, kv_heads, group_size, pair_rows)
    stats_final = lax.scan(
        stats_step,
        (jnp.full(stat_shape, NEG_SCORE, jnp.float32), jnp.zeros(stat_shape, jnp.float32)),
        starts,
    )[0]
    log_total = stats_final[0] + jnp.log(stats_final[1])

    def output_step(accum, start):
        key_tile, value_tile, scores, allowed = tile_at(start)
        probs_low = jnp.where(allowed, jnp.exp(scores - log_total[..., None]), 0.0).astype(
            jnp.bfloat16
        )
        return (
            accum
            + jnp.einsum(
                "shgqk,skhd->sqhgd", probs_low, value_tile, preferred_element_type=jnp.float32
            ),
            None,
        )

    head_shape = (seq_count, pair_rows, kv_heads, group_size, HD)
    attended = lax.scan(output_step, jnp.zeros(head_shape, jnp.float32), starts)[0]
    attn_low = attended.reshape(local_rows, q_width).astype(jnp.bfloat16)
    resid = tokens_f + lax.psum_scatter(
        jnp.dot(attn_low, w_proj, preferred_element_type=jnp.float32).astype(jnp.bfloat16),
        "tp",
        scatter_dimension=0,
        tiled=True,
    ).astype(jnp.float32)
    gain_ffn, w_gu, w_dn = (
        lax.all_gather(ffn_gain, "ctx", axis=0, tiled=True),
        lax.all_gather(jnp.concatenate([w_gate, w_up], axis=1), "ctx", axis=0, tiled=True),
        lax.all_gather(w_down, "ctx", axis=1, tiled=True),
    )
    normal_two_f, norm_two_back = jax.vjp(normed, resid, gain_ffn.astype(jnp.float32))
    normal_two = normal_two_f.astype(jnp.bfloat16)
    rows_two = lax.all_gather(normal_two, "tp", axis=0, tiled=True)
    gate_up = jnp.dot(rows_two, w_gu, preferred_element_type=jnp.float32)
    gate = gate_up[:, :ff_local]
    up_proj = gate_up[:, ff_local:]
    sigmoid_gate = jax.nn.sigmoid(gate)
    silu_gate = gate * sigmoid_gate
    hidden = (silu_gate * up_proj).astype(jnp.bfloat16)
    out = (
        resid
        + sent_and_summed(
            jnp.dot(hidden, w_dn, preferred_element_type=jnp.float32).astype(jnp.bfloat16), "tp", 0
        )
    ).astype(jnp.bfloat16)
    grad_rows = lax.all_gather(out_grad, "tp", axis=0, tiled=True)
    grad_hidden = contract_last(grad_rows, w_dn)
    grad_gate = grad_hidden * up_proj * (sigmoid_gate * (1.0 + gate * (1.0 - sigmoid_gate)))
    grad_up = grad_hidden * silu_gate
    grad_gu = jnp.concatenate([grad_gate, grad_up], axis=1).astype(jnp.bfloat16)
    mlp_grads = jnp.concatenate(
        [contract_first(rows_two, grad_gu), contract_first(grad_rows, hidden)], axis=1
    )
    mlp_early = send_grads(mlp_grads)
    grad_norm_two = sent_and_summed(contract_last(grad_gu, w_gu).astype(jnp.bfloat16), "tp", 0)
    grad_resid_norm, grad_gain_ffn = norm_two_back(grad_norm_two)
    grad_resid = out_grad.astype(jnp.float32) + grad_resid_norm
    branch_rows = lax.all_gather(grad_resid.astype(jnp.bfloat16), "tp", axis=0, tiled=True)
    grad_attn_low = contract_last(branch_rows, w_proj).astype(jnp.bfloat16)
    grad_out_cols = contract_first(branch_rows, attn_low)
    grad_attn_heads = grad_attn_low.reshape(head_shape)
    delta = jnp.transpose(
        jnp.sum(grad_attn_heads.astype(jnp.float32) * attended, axis=-1), (0, 2, 3, 1)
    )

    def scores_grad(probs, grad_probs, delta_here):
        return (probs * (grad_probs - delta_here[..., None])).astype(jnp.bfloat16)

    def grad_step(carry, start):
        accum, key_grad_all, value_grad_all = carry
        key_tile, value_tile, scores, allowed = tile_at(start)
        probs = jnp.where(allowed, jnp.exp(scores - log_total[..., None]), 0.0)
        probs_low = probs.astype(jnp.bfloat16)
        grad_value = jnp.einsum(
            "shgqk,sqhgd->skhd", probs_low, grad_attn_heads, preferred_element_type=jnp.float32
        )
        grad_probs = jnp.einsum(
            "sqhgd,skhd->shgqk", grad_attn_heads, value_tile, preferred_element_type=jnp.float32
        )
        grad_scores = scores_grad(probs, grad_probs, delta)
        accum = (
            accum
            + jnp.einsum(
                "shgqk,skhd->sqhgd", grad_scores, key_tile, preferred_element_type=jnp.float32
            )
            * score_scale
        )
        grad_key = (
            jnp.einsum(
                "shgqk,sqhgd->skhd", grad_scores, query_low, preferred_element_type=jnp.float32
            )
            * score_scale
        )
        key_grad_all = lax.dynamic_update_slice_in_dim(
            key_grad_all, grad_key.reshape(seq_count, key_block, k_width), start, 1
        )
        value_grad_all = lax.dynamic_update_slice_in_dim(
            value_grad_all, grad_value.reshape(seq_count, key_block, k_width), start, 1
        )
        return ((accum, key_grad_all, value_grad_all), None)

    kv_zero = jnp.zeros((seq_count, seq_keys, k_width), jnp.float32)
    grad_query, key_grad_all, value_grad_all = lax.scan(
        grad_step, (jnp.zeros(head_shape, jnp.float32), kv_zero, kv_zero), starts
    )[0]
    grad_keys, grad_values = (
        lax.psum_scatter(
            key_grad_all.astype(jnp.bfloat16), "ctx", scatter_dimension=1, tiled=True
        ).astype(jnp.float32),
        lax.psum_scatter(
            value_grad_all.astype(jnp.bfloat16), "ctx", scatter_dimension=1, tiled=True
        ).astype(jnp.float32),
    )
    grad_query_pre, grad_gain_query = query_back(grad_query.reshape(local_rows, q_heads, HD))
    grad_key_pre, grad_gain_key = key_back(grad_keys.reshape(local_rows, kv_heads, HD))
    grad_qkv = jnp.concatenate(
        [
            grad_query_pre.reshape(local_rows, q_width),
            grad_key_pre.reshape(local_rows, k_width),
            grad_values.reshape(local_rows, k_width),
        ],
        axis=1,
    ).astype(jnp.bfloat16)
    attn_grads = jnp.concatenate([contract_first(rows_one, grad_qkv), grad_out_cols], axis=1)
    grad_norm_one = sent_and_summed(contract_last(grad_qkv, w_qkv).astype(jnp.bfloat16), "tp", 0)
    grad_input_norm, grad_gain_attn = norm_one_back(grad_norm_one)
    grad_x = (grad_resid + grad_input_norm).astype(jnp.bfloat16)
    gain_sums = lax.psum(
        (grad_gain_attn, grad_gain_query, grad_gain_key, grad_gain_ffn), ("ctx", "tp")
    )
    d_share = gain_sums[0].shape[0] // ctx_count
    h_share = gain_sums[1].shape[0] // ctx_count
    attn_owned = send_grads(attn_grads)
    return (
        out,
        grad_x,
        lax.dynamic_slice_in_dim(gain_sums[0], ctx_rank * d_share, d_share),
        attn_owned[:, :q_width],
        attn_owned[:, q_width : q_width + k_width],
        attn_owned[:, q_width + k_width : q_width + 2 * k_width],
        lax.dynamic_slice_in_dim(gain_sums[1], ctx_rank * h_share, h_share),
        lax.dynamic_slice_in_dim(gain_sums[2], ctx_rank * h_share, h_share),
        jnp.transpose(attn_owned[:, q_width + 2 * k_width :]),
        lax.dynamic_slice_in_dim(gain_sums[3], ctx_rank * d_share, d_share),
        mlp_early[:, :ff_local],
        mlp_early[:, ff_local : 2 * ff_local],
        jnp.transpose(mlp_early[:, 2 * ff_local :]),
    )


def solution(mesh):
    in_specs = (
        P(("ctx", "tp"), None),
        P(),
        P(),
        P("ctx"),
        P("ctx", "tp"),
        P("ctx", "tp"),
        P("ctx", "tp"),
        P("ctx"),
        P("ctx"),
        P("tp", "ctx"),
        P("ctx"),
        P("ctx", "tp"),
        P("ctx", "tp"),
        P("tp", "ctx"),
        P(("ctx", "tp"), None),
    )
    out_specs = (
        P(("ctx", "tp"), None),
        P(("ctx", "tp"), None),
        P("ctx"),
        P("ctx", "tp"),
        P("ctx", "tp"),
        P("ctx", "tp"),
        P("ctx"),
        P("ctx"),
        P("tp", "ctx"),
        P("ctx"),
        P("ctx", "tp"),
        P("ctx", "tp"),
        P("tp", "ctx"),
    )
    return jax.shard_map(
        per_device, mesh=mesh, in_specs=in_specs, out_specs=out_specs, check_vma=False
    )
```

profile of v0, /device:TPU:1, one launch (start us, length us, event | category | flops | bytes accessed | tf_op | source)
XLA Modules:
  0.0 1124.1 jit_solution(7905820449707120170)
XLA Ops:
  14.7 30.3 %all-reduce.11 = (bf16[1024]{0:T(1024)(128)(2,1)S(1)}, bf16[128]{0:T(256)(128)(2,1)S(1)}, bf16[128]{0:T(256)(128)(2,1)S(1)}, bf16[1024]{0:T(1024)(128)(2,1)}) all-reduce(bf16[1024]{0:T(1024)(128)(2,1)S(1)} %dynamic-update-slice, bf16[128]{0:T(256)(128)(2,1)S(1)} %dynamic-update-slice.1, ...), channel_id=1, replica_groups=mesh['ctx'=16,'tp'=8] {'ctx'}, use_global_device_ids=true, to_apply=%add.6 | all-reduce | flops 2304 | bytes 9216
  52.0 8.8 gather_fusion.2
  60.9 9.1 gather_fusion.4
  70.9 33.8 %all-gather.9.cloned.1.call-done = bf16[1024,1024]{1,0:T(8,128)(2,1)} async-done(((bf16[128,1024]{1,0:T(8,128)(2,1)}), bf16[1024,1024]{1,0:T(8,128)(2,1)}) %all-gather.9.cloned.1.call-update) | async-done | bytes 2097168 | tf_op jit(solution)/shard_map/all_gather | solution.py:130
  112.1 9.1 gather_fusion.3
  124.0 33.8 %gather_fusion = s32[4096]{0:T(1024)S(1)} fusion(s32[16,2]{0,1:T(2,128)S(1)} %copy-done, s32[4096]{0:T(1024)S(1)} %bitcast.382), kind=kCustom, calls=%fused_computation | custom fusion | bytes 65536 | tf_op jit(solution)/shard_map/gather | solution.py:96
  157.9 15.8 %gather_fusion.1 = s32[4096,4]{1,0:T(8,128)} fusion(s32[4,4096]{0,1:T(8,128)} %copy.155, s32[4096]{0:T(1024)S(1)} %broadcast_clamp_fusion), kind=kCustom, calls=%fused_computation.1 | custom fusion | bytes 147456 | tf_op jit(solution)/shard_map/gather | solution.py:99
  181.5 22.6 %all_gather.49 = bf16[256,1024]{0,1:T(8,128)(2,1)} all-gather(bf16[256,64]{0,1:T(8,128)(2,1)S(1)} %copy-done.40), channel_id=1, replica_groups=mesh['ctx'=16,'tp'=8] {'ctx'}, dimensions={1}, use_global_device_ids=true | all-gather | bytes 557056 | tf_op jit(solution)/shard_map/all_gather | solution.py:125
  213.8 56.3 %while.42 = (s32[]{:T(128)}, f32[4,1,2,256]{3,2,0,1:T(2,128)S(1)}, f32[4,1,2,256]{3,2,0,1:T(2,128)S(1)}, s32[8]{0:T(128)}, s32[4,4096]{1,0:T(4,128)S(1)}, /*inde...) while((s32[]{:T(128)}, f32[4,1,2,256]{3,2,0,1:T(2,128)S(1)}, ...), condition=%wide.wide.region_8.9_spmd.clone, body=%wide.wide.region_5.8_spmd.clone.sunk | while | flops 278407168 | bytes 11155674 | solution.py:179
  270.2 54.3 %while.43 = (s32[]{:T(128)}, f32[4,256,1,2,128]{1,4,3,0,2:T(8,128)S(1)}, s32[8]{0:T(128)}, bf16[4,4096,1,128]{3,1,0,2:T(8,128)(2,1)}, s32[4,4096]{1,0:T(4,128)S(...) while((s32[]{:T(128)}, ...), condition=%wide.wide.region_10.11_spmd.clone, body=%wide.wide.region_9.10_spmd.clone.sunk | while | flops 543162368 | bytes 4767452 | solution.py:200
  328.5 68.6 %reduce-scatter.10.cloned.1.call-done = bf16[128,1024]{1,0:T(8,128)(2,1)} async-done(((bf16[1024,1024]{1,0:T(8,128)(2,1)}), bf16[128,1024]{1,0:T(8,128)(2,1)}) %reduce-scatter.10.cloned.1.call-update) | async-done | bytes 262160 | tf_op jit(solution)/shard_map/reduce_scatter | solution.py:202
  400.8 23.9 %all_gather.53 = bf16[384,1024]{0,1:T(8,128)(2,1)S(1)} all-gather(bf16[384,64]{0,1:T(8,128)(2,1)} %param.34), channel_id=1, replica_groups=mesh['ctx'=16,'tp'=8] {'ctx'}, dimensions={1}, use_global_device_ids=true | all-gather | bytes 835584 | tf_op jit(solution)/shard_map/all_gather | solution.py:211
  424.7 9.1 all-gather.19.cloned.1.call-done
  433.8 55.7 %all-gather.17.cloned.1.call-done = bf16[1024,1024]{1,0:T(8,128)(2,1)} async-done(((bf16[128,1024]{1,0:T(8,128)(2,1)}), bf16[1024,1024]{1,0:T(8,128)(2,1)}) %all-gather.17.cloned.1.call-update) | async-done | bytes 2097168 | tf_op jit(solution)/shard_map/all_gather | solution.py:215
  495.0 48.6 %all-gather.21.cloned.1.call-done = bf16[1024,1024]{1,0:T(8,128)(2,1)} async-done(((bf16[128,1024]{1,0:T(8,128)(2,1)}), bf16[1024,1024]{1,0:T(8,128)(2,1)}) %all-gather.21.cloned.1.call-update) | async-done | bytes 2097168 | tf_op jit(solution)/shard_map/all_gather | solution.py:228
  550.7 30.0 %all_to_all.15 = bf16[8,128,1024]{2,1,0:T(8,128)(2,1)S(1)} all-to-all(bf16[8,128,1024]{2,1,0:T(8,128)(2,1)S(1)} %bitcast.393), channel_id=1, replica_groups=mesh['ctx'=16,'tp'=8] {'tp'}, dimensions={0} | all-to-all | bytes 4194304 | tf_op jit(solution)/shard_map/all_to_all | solution.py:20
  583.5 52.6 %all-gather.23.cloned.1.call-done = bf16[1024,1024]{1,0:T(8,128)(2,1)} async-done(((bf16[128,1024]{1,0:T(8,128)(2,1)}), bf16[1024,1024]{1,0:T(8,128)(2,1)}) %all-gather.23.cloned.1.call-update) | async-done | bytes 2097168 | tf_op jit(solution)/shard_map/all_gather | solution.py:240
  648.6 176.8 %while.44 = (s32[]{:T(128)}, f32[4,256,1,2,128]{1,4,3,0,2:T(8,128)S(1)}, bf16[4,4096,128]{2,1,0:T(8,128)(2,1)}, bf16[4,4096,128]{2,1,0:T(8,128)(2,1)}, s32[8]{0:...) while((s32[]{:T(128)}, ...), condition=%wide.wide.region_18.19_spmd.clone, body=%wide.wide.region_17.18_spmd.clone.sunk | while | flops 1355546624 | bytes 29423888 | solution.py:285
  659.7 5.6 dynamic_update_slice.12
  682.0 5.6 dynamic_update_slice.12
  704.3 5.6 dynamic_update_slice.12
  709.8 5.6 dynamic_update_slice.13
  726.5 5.6 dynamic_update_slice.12
  748.8 5.6 dynamic_update_slice.12
  771.1 5.6 dynamic_update_slice.12
  793.3 5.6 dynamic_update_slice.12
  798.9 5.6 dynamic_update_slice.13
  854.6 41.9 %reduce-scatter.14.cloned.1.call-done = bf16[4,256,128]{2,1,0:T(8,128)(2,1)} async-done(((bf16[4,4096,128]{2,1,0:T(8,128)(2,1)}), bf16[4,256,128]{2,1,0:T(8,128)(2,1)}) %reduce-scatter.14.cloned.1.call-update) | async-done | bytes 262160 | tf_op jit(solution)/shard_map/reduce_scatter | solution.py:292
  897.6 64.9 %reduce-scatter.12.cloned.1.call-done = bf16[4,256,128]{2,1,0:T(8,128)(2,1)} async-done(((bf16[4,4096,128]{2,1,0:T(8,128)(2,1)}), bf16[4,256,128]{2,1,0:T(8,128)(2,1)}) %reduce-scatter.12.cloned.1.call-update) | async-done | bytes 262160 | tf_op jit(solution)/shard_map/reduce_scatter | solution.py:289
  976.5 6.8 all-to-all-start.2
  986.1 45.8 %reduce-scatter.18.cloned.1.call-done = bf16[64,1152]{1,0:T(8,128)(2,1)} async-done(((bf16[1024,1152]{1,0:T(8,128)(2,1)}), bf16[64,1152]{1,0:T(8,128)(2,1)}) %reduce-scatter.18.cloned.1.call-update) | async-done | bytes 147472
  1040.3 68.1 %all-reduce.10 = (f32[1024]{0:T(1024)S(1)}, f32[128]{0:T(128)S(1)}, f32[128]{0:T(128)S(1)}, f32[1024]{0:T(1024)S(1)}) all-reduce(f32[1024]{0:T(1024)S(1)} %get-tuple-element.576, f32[128]{0:T(128)S(1)} %get-tuple-element.574, f32[128]{0:T(128)S(1)} %get-tuple-element.570, ...), channel_id=1, replica_groups=mesh['ctx'=16,'tp'=8] {'ctx','tp'}, use_global_device_ids=true, to_apply=%region_26.27 | all-reduce | flops 2304 | bytes 18432 | tf_op jit(solution)/shard_map/psum | solution.py:310
  (493 shorter events, 330.1 us)
Async XLA Ops:
  7.2 44.9 %copy-start = (s32[16,2]{0,1:T(2,128)S(1)}, s32[16,2]{0,1:T(2,128)}, u32[]{:S(2)}) copy-start(s32[16,2]{0,1:T(2,128)} %param.22) | copy-start | bytes 388
  7.2 63.7 %all-gather.11.cloned.1.call-start = ((), (), s32[]{:S(2)}) async-start(), calls=%async_computation.9 | async-start | bytes 1114112 | tf_op jit(solution)/shard_map/all_gather | solution.py:122
  8.7 96.0 %all-gather.9.cloned.1.call-start = ((), (), s32[]{:S(2)}) async-start(), calls=%async_computation.8 | async-start | bytes 2359296 | tf_op jit(solution)/shard_map/all_gather | solution.py:130
  49.0 164.8 %all-gather.15.cloned.1.call-start = ((), (), s32[]{:S(2)}) async-start(), calls=%async_computation.11 | async-start | bytes 4456448 | tf_op jit(solution)/shard_map/all_gather | solution.py:147
  49.1 59.0 %copy-start.41 = (f32[128]{0:T(128)}, f32[128]{0:T(128)S(1)}, u32[]{:S(2)}) copy-start(f32[128]{0:T(128)S(1)} %convert_element_type.135) | copy-start | bytes 1540
  70.1 51.2 %copy-start.32 = (s32[1024]{0:T(1024)}, s32[1024]{0:T(1024)S(1)}, u32[]{:S(2)}) copy-start(s32[1024]{0:T(1024)S(1)} %get-tuple-element.1194) | copy-start | bytes 12292
  107.8 99.0 %copy-start.3 = (f32[1024,512]{0,1:T(8,128)}, f32[1024,512]{0,1:T(8,128)S(1)}, u32[]{:S(2)}) copy-start(f32[1024,512]{0,1:T(8,128)S(1)} %fusion.161) | copy-start | bytes 6291460
  112.0 158.2 %all-gather.13.cloned.1.call-start = ((), (), s32[]{:S(2)}) async-start(), calls=%async_computation.10 | async-start | bytes 4456448 | tf_op jit(solution)/shard_map/all_gather | solution.py:148
  121.2 36.6 %copy-start.34 = (s32[1024]{0:T(1024)}, s32[1024]{0:T(1024)S(1)}, u32[]{:S(2)}) copy-start(s32[1024]{0:T(1024)S(1)} %gather_fusion.3) | copy-start | bytes 12292
  157.9 23.7 %copy-start.40 = (bf16[256,64]{0,1:T(8,128)(2,1)S(1)}, bf16[256,64]{0,1:T(8,128)(2,1)}, u32[]{:S(2)}) copy-start(bf16[256,64]{0,1:T(8,128)(2,1)} %param.30) | copy-start | bytes 98308
  213.6 183.5 %reduce-scatter.10.cloned.1.call-start = ((), (), s32[]{:S(2)}) async-start(), calls=%async_computation.12 | async-start | bytes 2359296 | tf_op jit(solution)/shard_map/reduce_scatter | solution.py:202
  213.8 56.4 %copy-start.13 = (f32[4,256,1,2,128]{1,4,3,0,2:T(8,128)S(1)}, f32[4,256,1,2,128]{1,4,3,0,2:T(8,128)}, u32[]{:S(2)}) copy-start(f32[4,256,1,2,128]{1,4,3,0,2:T(8,128)} %custom-call.10) | copy-start | bytes 3145732
  325.5 71.5 %copy-start.5 = (bf16[128,1024]{1,0:T(8,128)(2,1)S(1)}, bf16[128,1024]{1,0:T(8,128)(2,1)}, u32[]{:S(2)}) copy-start(bf16[128,1024]{1,0:T(8,128)(2,1)} %param.21) | copy-start | bytes 786436
  327.7 106.2 %all-gather.19.cloned.1.call-start = ((), (), s32[]{:S(2)}) async-start(), calls=%async_computation.14 | async-start | bytes 1671168 | tf_op jit(solution)/shard_map/all_gather | solution.py:210
  328.4 161.1 %all-gather.17.cloned.1.call-start = ((), (), s32[]{:S(2)}) async-start(), calls=%async_computation.13 | async-start | bytes 2359296 | tf_op jit(solution)/shard_map/all_gather | solution.py:215
  400.0 143.7 %all-gather.21.cloned.1.call-start = ((), (), s32[]{:S(2)}) async-start(), calls=%async_computation.15 | async-start | bytes 2359296 | tf_op jit(solution)/shard_map/all_gather | solution.py:228
  400.7 235.4 %all-gather.23.cloned.1.call-start = ((), (), s32[]{:S(2)}) async-start(), calls=%async_computation.16 | async-start | bytes 2359296 | tf_op jit(solution)/shard_map/all_gather | solution.py:240
  424.7 118.9 %copy-start.24 = (bf16[384,1024]{0,1:T(8,128)(2,1)}, bf16[384,1024]{0,1:T(8,128)(2,1)S(1)}, u32[]{:S(2)}) copy-start(bf16[384,1024]{0,1:T(8,128)(2,1)S(1)} %all_gather.53) | copy-start | bytes 2359300
  582.5 56.8 %copy-start.47 = (f32[128]{0:T(128)}, f32[128]{0:T(128)S(1)}, u32[]{:S(2)}) copy-start(f32[128]{0:T(128)S(1)} %multiply_multiply_fusion.4) | copy-start | bytes 1540
  583.4 313.1 %reduce-scatter.14.cloned.1.call-start = ((), (), s32[]{:S(2)}) async-start(), calls=%async_computation.18 | async-start | bytes 4456448 | tf_op jit(solution)/shard_map/reduce_scatter | solution.py:292
  825.5 137.0 %reduce-scatter.12.cloned.1.call-start = ((), (), s32[]{:S(2)}) async-start(), calls=%async_computation.17 | async-start | bytes 4456448 | tf_op jit(solution)/shard_map/reduce_scatter | solution.py:289
  826.2 205.7 %reduce-scatter.18.cloned.1.call-start = ((), (), s32[]{:S(2)}) async-start(), calls=%async_computation.20 | async-start | bytes 2506752
  841.1 135.5 %all-to-all-start = ((bf16[8,128,1024]{2,1,0:T(8,128)(2,1)}), bf16[8,128,1024]{2,1,0:T(8,128)(2,1)}, u32[]{:S(2)}, u32[]{:S(2)}) async-start(bf16[8,128,1024]{2,1,0:T(8,128)(2,1)} %bitcast.391), calls=%async_computation.1 | async-start | bytes 4194304 | tf_op jit(solution)/shard_map/all_to_all | solution.py:20
  845.4 267.7 %reduce-scatter.16.cloned.1.call-start = ((), (), s32[]{:S(2)}) async-start(), calls=%async_computation.19 | async-start | bytes 1671168
  854.6 110.9 %copy-start.15 = (f32[1024,1,64]{0,2,1:T(8,128)S(1)}, f32[1024,1,64]{0,2,1:T(8,128)}, u32[]{:S(2)}) copy-start(f32[1024,1,64]{0,2,1:T(8,128)} %get-tuple-element.686) | copy-start | bytes 786436
  897.5 69.8 %copy-start.42 = (f32[128]{0:T(128)S(1)}, f32[128]{0:T(128)}, u32[]{:S(2)}) copy-start(f32[128]{0:T(128)} %copy-done.41) | copy-start | bytes 1540
  976.5 62.4 %all-to-all-start.2 = ((bf16[8,128,1024]{2,1,0:T(8,128)(2,1)}), bf16[8,128,1024]{2,1,0:T(8,128)(2,1)S(1)}, u32[]{:S(2)}, u32[]{:S(2)}) async-start(bf16[8,128,1024]{2,1,0:T(8,128)(2,1)} %bitcast.392), calls=%async_computation.5 | async-start | bytes 4194304 | tf_op jit(solution)/shard_map/all_to_all | solution.py:20
  1035.5 75.2 %copy-start.51 = (f32[128]{0:T(128)S(1)}, f32[128]{0:T(128)}, u32[]{:S(2)}) copy-start(f32[128]{0:T(128)} %copy-done.50) | copy-start | bytes 1540
  1035.5 75.2 %copy-start.9 = (f32[128,1024]{1,0:T(8,128)S(1)}, f32[128,1024]{1,0:T(8,128)}, u32[]{:S(2)}) copy-start(f32[128,1024]{1,0:T(8,128)} %copy-done.8) | copy-start | bytes 1572868
  1035.5 75.2 %copy-start.11 = (bf16[128,1024]{1,0:T(8,128)(2,1)S(1)}, bf16[128,1024]{1,0:T(8,128)(2,1)}, u32[]{:S(2)}) copy-start(bf16[128,1024]{1,0:T(8,128)(2,1)} %reduce-scatter.10.cloned.1.call-done) | copy-start | bytes 786436
  1035.5 75.3 %copy-start.17 = (bf16[128,1024]{1,0:T(8,128)(2,1)S(1)}, bf16[128,1024]{1,0:T(8,128)(2,1)}, u32[]{:S(2)}) copy-start(bf16[128,1024]{1,0:T(8,128)(2,1)} %param.35) | copy-start | bytes 786436
  1035.5 75.3 %copy-start.48 = (f32[128]{0:T(128)S(1)}, f32[128]{0:T(128)}, u32[]{:S(2)}) copy-start(f32[128]{0:T(128)} %copy-done.47) | copy-start | bytes 1540
  (45 other events, 111.3 us)
Sparse Core Ops, SparseCore 0:
  10.3 36.2 all-gather.10
  49.5 55.1 all-gather.8
  112.1 36.1 all-gather.14
  213.7 33.6 all-gather.12
  327.8 69.2 reduce-scatter.9
  399.2 34.5 all-gather.18
  436.7 52.7 all-gather.16
  491.9 51.7 all-gather.20
  583.5 52.5 all-gather.22
  825.6 70.8 reduce-scatter.13
  898.9 63.5 reduce-scatter.11
  964.7 67.1 reduce-scatter.17
  1034.3 60.6 reduce-scatter.15
where the time goes:
time: 1140 us; the launch traced here: 1120 us
  waiting for transfers between devices  423 us (37%)
  local copies, waits for them, and re-layouts  248 us (22%)
  blocking collectives  175 us (15%)
  matrix products  135 us (12%)
  other arithmetic  66.5 us (6%)
  loops' own time  47.7 us (4%)
  between operations  16.8 us (1%)
  starting transfers between devices  12.1 us (1%)
    reduce_scatter x1, waiting for transfers between devices, per_device(): lax.psum_scatter(jnp.dot(attn_low, w_proj, preferred_element_type=jnp.flo...  68.6 us
    psum x1, blocking collectives, per_device(): lax.psum((grad_gain_attn, grad_gain_query, grad_gain_key, grad_gain_ffn),...  68.1 us
    reduce_scatter x1, waiting for transfers between devices, per_device(): lax.psum_scatter(key_grad_all.astype(jnp.bfloat16), 'ctx', scatter_dimens...  64.9 us
    all_gather x1, waiting for transfers between devices, per_device(): rows_two = lax.all_gather(normal_two, 'tp', axis=0, tiled=True)  55.7 us
    all_gather x1, waiting for transfers between devices, per_device(): lax.all_gather(grad_resid.astype(jnp.bfloat16), 'tp', axis=0, tiled=True)  52.6 us
    all_gather x1, waiting for transfers between devices, per_device(): grad_rows = lax.all_gather(out_grad, 'tp', axis=0, tiled=True)  48.6 us
    unnamed x15, waiting for transfers between devices  47.4 us
    dynamic_update_slice x8, local copies, waits for them, and re-layouts, grad_step(): lax.dynamic_update_slice_in_dim(key_grad_all, grad_key.reshape(seq_count,...  43.9 us
  transfers between devices with their start and end apart: 15, of which 9 were waited for; matrix products, arithmetic and copies ran while one was open for 18% of the time, Pallas kernels for 0%

commit v1 on v0

--- a/solution.py
+++ b/solution.py
@@ -308,7 +308,7 @@
     grad_input_norm, grad_gain_attn = norm_one_back(grad_norm_one)
     grad_x = (grad_resid + grad_input_norm).astype(jnp.bfloat16)
     gain_sums = lax.psum(
-        (grad_gain_attn, grad_gain_query, grad_gain_key, grad_gain_ffn), ("ctx", "tp")
+        lax.psum((grad_gain_attn, grad_gain_query, grad_gain_key, grad_gain_ffn), "ctx"), "tp"
     )
     d_share = gain_sums[0].shape[0] // ctx_count
     h_share = gain_sums[1].shape[0] // ctx_count

time: 1140 us -> 1130 us (level)
  blocking collectives: 175 us -> 159 us
    psum x1, blocking collectives: 68.1 us -> 31.5 us  [per_device(): lax.psum((grad_gain_attn, grad_gain_query, grad_gain_key, grad_gain_ffn),...]
    psum x0 -> x1, blocking collectives: none -> 21.2 us  [per_device(): lax.psum(lax.psum((grad_gain_attn, grad_gain_query, grad_gain_key, grad_g...]
  transfers between devices with their start and end apart: 15 -> 15, of which waited for: 9 -> 9; matrix products, arithmetic and copies ran while one was open for 18% -> 19% of each run, Pallas kernels for 0% -> 0%
where the time goes in v1:
time: 1130 us; the launch traced here: 1110 us
  waiting for transfers between devices  423 us (37%)
  local copies, waits for them, and re-layouts  248 us (22%)
  blocking collectives  159 us (14%)
  matrix products  135 us (12%)
  other arithmetic  66.6 us (6%)
  loops' own time  47.7 us (4%)
  between operations  16.9 us (1%)
  starting transfers between devices  12.1 us (1%)
    reduce_scatter x1, waiting for transfers between devices, per_device(): lax.psum_scatter(jnp.dot(attn_low, w_proj, preferred_element_type=jnp.flo...  68.6 us
    reduce_scatter x1, waiting for transfers between devices, per_device(): lax.psum_scatter(key_grad_all.astype(jnp.bfloat16), 'ctx', scatter_dimens...  65 us
    all_gather x1, waiting for transfers between devices, per_device(): rows_two = lax.all_gather(normal_two, 'tp', axis=0, tiled=True)  55.7 us
    all_gather x1, waiting for transfers between devices, per_device(): lax.all_gather(grad_resid.astype(jnp.bfloat16), 'tp', axis=0, tiled=True)  52.7 us
    all_gather x1, waiting for transfers between devices, per_device(): grad_rows = lax.all_gather(out_grad, 'tp', axis=0, tiled=True)  48.6 us
    unnamed x15, waiting for transfers between devices  47.3 us
    dynamic_update_slice x8, local copies, waits for them, and re-layouts, grad_step(): lax.dynamic_update_slice_in_dim(key_grad_all, grad_key.reshape(seq_count,...  43.9 us
    dynamic_update_slice x8, local copies, waits for them, and re-layouts, grad_step(): lax.dynamic_update_slice_in_dim(value_grad_all, grad_value.reshape(seq_co...  43.8 us
  transfers between devices with their start and end apart: 15, of which 9 were waited for; matrix products, arithmetic and copies ran while one was open for 19% of the time, Pallas kernels for 0%

profile of v1, /device:TPU:1, one launch (start us, length us, event | category | flops | bytes accessed | tf_op | source)
XLA Modules:
  0.0 1108.7 jit_solution(3416146428077249666)
XLA Ops:
  14.7 30.3 %all-reduce.12 = (bf16[1024]{0:T(1024)(128)(2,1)S(1)}, bf16[128]{0:T(256)(128)(2,1)S(1)}, bf16[128]{0:T(256)(128)(2,1)S(1)}, bf16[1024]{0:T(1024)(128)(2,1)}) all-reduce(bf16[1024]{0:T(1024)(128)(2,1)S(1)} %dynamic-update-slice, bf16[128]{0:T(256)(128)(2,1)S(1)} %dynamic-update-slice.1, ...), channel_id=1, replica_groups=mesh['ctx'=16,'tp'=8] {'ctx'}, use_global_device_ids=true, to_apply=%add.6 | all-reduce | flops 2304 | bytes 9216
  52.0 8.8 gather_fusion.2
  60.9 9.1 gather_fusion.4
  70.9 33.8 %all-gather.9.cloned.1.call-done = bf16[1024,1024]{1,0:T(8,128)(2,1)} async-done(((bf16[128,1024]{1,0:T(8,128)(2,1)}), bf16[1024,1024]{1,0:T(8,128)(2,1)}) %all-gather.9.cloned.1.call-update) | async-done | bytes 2097168 | tf_op jit(solution)/shard_map/all_gather | solution.py:130
  112.1 9.1 gather_fusion.3
  124.0 33.8 %gather_fusion = s32[4096]{0:T(1024)S(1)} fusion(s32[16,2]{0,1:T(2,128)S(1)} %copy-done, s32[4096]{0:T(1024)S(1)} %bitcast.382), kind=kCustom, calls=%fused_computation | custom fusion | bytes 65536 | tf_op jit(solution)/shard_map/gather | solution.py:96
  157.9 15.8 %gather_fusion.1 = s32[4096,4]{1,0:T(8,128)} fusion(s32[4,4096]{0,1:T(8,128)} %copy.155, s32[4096]{0:T(1024)S(1)} %broadcast_clamp_fusion), kind=kCustom, calls=%fused_computation.1 | custom fusion | bytes 147456 | tf_op jit(solution)/shard_map/gather | solution.py:99
  181.5 22.6 %all_gather.49 = bf16[256,1024]{0,1:T(8,128)(2,1)} all-gather(bf16[256,64]{0,1:T(8,128)(2,1)S(1)} %copy-done.40), channel_id=1, replica_groups=mesh['ctx'=16,'tp'=8] {'ctx'}, dimensions={1}, use_global_device_ids=true | all-gather | bytes 557056 | tf_op jit(solution)/shard_map/all_gather | solution.py:125
  213.8 56.3 %while.42 = (s32[]{:T(128)}, f32[4,1,2,256]{3,2,0,1:T(2,128)S(1)}, f32[4,1,2,256]{3,2,0,1:T(2,128)S(1)}, s32[8]{0:T(128)}, s32[4,4096]{1,0:T(4,128)S(1)}, /*inde...) while((s32[]{:T(128)}, f32[4,1,2,256]{3,2,0,1:T(2,128)S(1)}, ...), condition=%wide.wide.region_8.9_spmd.clone, body=%wide.wide.region_5.8_spmd.clone.sunk | while | flops 278407168 | bytes 11155674 | solution.py:179
  270.2 54.3 %while.43 = (s32[]{:T(128)}, f32[4,256,1,2,128]{1,4,3,0,2:T(8,128)S(1)}, s32[8]{0:T(128)}, bf16[4,4096,1,128]{3,1,0,2:T(8,128)(2,1)}, s32[4,4096]{1,0:T(4,128)S(...) while((s32[]{:T(128)}, ...), condition=%wide.wide.region_10.11_spmd.clone, body=%wide.wide.region_9.10_spmd.clone.sunk | while | flops 543162368 | bytes 4767452 | solution.py:200
  328.5 68.6 %reduce-scatter.10.cloned.1.call-done = bf16[128,1024]{1,0:T(8,128)(2,1)} async-done(((bf16[1024,1024]{1,0:T(8,128)(2,1)}), bf16[128,1024]{1,0:T(8,128)(2,1)}) %reduce-scatter.10.cloned.1.call-update) | async-done | bytes 262160 | tf_op jit(solution)/shard_map/reduce_scatter | solution.py:202
  400.8 23.9 %all_gather.53 = bf16[384,1024]{0,1:T(8,128)(2,1)S(1)} all-gather(bf16[384,64]{0,1:T(8,128)(2,1)} %param.34), channel_id=1, replica_groups=mesh['ctx'=16,'tp'=8] {'ctx'}, dimensions={1}, use_global_device_ids=true | all-gather | bytes 835584 | tf_op jit(solution)/shard_map/all_gather | solution.py:211
  424.7 9.1 all-gather.19.cloned.1.call-done
  433.8 55.7 %all-gather.17.cloned.1.call-done = bf16[1024,1024]{1,0:T(8,128)(2,1)} async-done(((bf16[128,1024]{1,0:T(8,128)(2,1)}), bf16[1024,1024]{1,0:T(8,128)(2,1)}) %all-gather.17.cloned.1.call-update) | async-done | bytes 2097168 | tf_op jit(solution)/shard_map/all_gather | solution.py:215
  495.0 48.6 %all-gather.21.cloned.1.call-done = bf16[1024,1024]{1,0:T(8,128)(2,1)} async-done(((bf16[128,1024]{1,0:T(8,128)(2,1)}), bf16[1024,1024]{1,0:T(8,128)(2,1)}) %all-gather.21.cloned.1.call-update) | async-done | bytes 2097168 | tf_op jit(solution)/shard_map/all_gather | solution.py:228
  550.6 29.9 %all_to_all.15 = bf16[8,128,1024]{2,1,0:T(8,128)(2,1)S(1)} all-to-all(bf16[8,128,1024]{2,1,0:T(8,128)(2,1)S(1)} %bitcast.393), channel_id=1, replica_groups=mesh['ctx'=16,'tp'=8] {'tp'}, dimensions={0} | all-to-all | bytes 4194304 | tf_op jit(solution)/shard_map/all_to_all | solution.py:20
  583.4 52.7 %all-gather.23.cloned.1.call-done = bf16[1024,1024]{1,0:T(8,128)(2,1)} async-done(((bf16[128,1024]{1,0:T(8,128)(2,1)}), bf16[1024,1024]{1,0:T(8,128)(2,1)}) %all-gather.23.cloned.1.call-update) | async-done | bytes 2097168 | tf_op jit(solution)/shard_map/all_gather | solution.py:240
  648.6 176.8 %while.44 = (s32[]{:T(128)}, f32[4,256,1,2,128]{1,4,3,0,2:T(8,128)S(1)}, bf16[4,4096,128]{2,1,0:T(8,128)(2,1)}, bf16[4,4096,128]{2,1,0:T(8,128)(2,1)}, s32[8]{0:...) while((s32[]{:T(128)}, ...), condition=%wide.wide.region_18.19_spmd.clone, body=%wide.wide.region_17.18_spmd.clone.sunk | while | flops 1355546624 | bytes 29423888 | solution.py:285
  659.7 5.6 dynamic_update_slice.12
  682.0 5.6 dynamic_update_slice.12
  687.5 5.6 dynamic_update_slice.13
  704.3 5.6 dynamic_update_slice.12
  726.5 5.6 dynamic_update_slice.12
  748.8 5.6 dynamic_update_slice.12
  754.3 5.6 dynamic_update_slice.13
  771.1 5.6 dynamic_update_slice.12
  854.4 41.9 %reduce-scatter.14.cloned.1.call-done = bf16[4,256,128]{2,1,0:T(8,128)(2,1)} async-done(((bf16[4,4096,128]{2,1,0:T(8,128)(2,1)}), bf16[4,256,128]{2,1,0:T(8,128)(2,1)}) %reduce-scatter.14.cloned.1.call-update) | async-done | bytes 262160 | tf_op jit(solution)/shard_map/reduce_scatter | solution.py:292
  897.4 65.0 %reduce-scatter.12.cloned.1.call-done = bf16[4,256,128]{2,1,0:T(8,128)(2,1)} async-done(((bf16[4,4096,128]{2,1,0:T(8,128)(2,1)}), bf16[4,256,128]{2,1,0:T(8,128)(2,1)}) %reduce-scatter.12.cloned.1.call-update) | async-done | bytes 262160 | tf_op jit(solution)/shard_map/reduce_scatter | solution.py:289
  976.5 6.8 all-to-all-start.2
  986.1 45.7 %reduce-scatter.18.cloned.1.call-done = bf16[64,1152]{1,0:T(8,128)(2,1)} async-done(((bf16[1024,1152]{1,0:T(8,128)(2,1)}), bf16[64,1152]{1,0:T(8,128)(2,1)}) %reduce-scatter.18.cloned.1.call-update) | async-done | bytes 147472
  1040.2 31.5 %all-reduce.10 = (f32[1024]{0:T(1024)S(1)}, f32[128]{0:T(128)S(1)}, f32[128]{0:T(128)S(1)}, f32[1024]{0:T(1024)S(1)}) all-reduce(f32[1024]{0:T(1024)S(1)} %get-tuple-element.576, f32[128]{0:T(128)S(1)} %get-tuple-element.574, f32[128]{0:T(128)S(1)} %get-tuple-element.570, ...), channel_id=1, replica_groups=mesh['ctx'=16,'tp'=8] {'ctx'}, use_global_device_ids=true, to_apply=%region_26.27 | all-reduce | flops 2304 | bytes 18432 | tf_op jit(solution)/shard_map/psum | solution.py:311
  1071.8 21.2 %all-reduce.11 = (f32[1024]{0:T(1024)S(1)}, f32[128]{0:T(128)S(1)}, f32[128]{0:T(128)S(1)}, f32[1024]{0:T(1024)S(1)}) all-reduce(f32[1024]{0:T(1024)S(1)} %get-tuple-element.650, f32[128]{0:T(128)S(1)} %get-tuple-element.651, f32[128]{0:T(128)S(1)} %get-tuple-element.652, ...), channel_id=1, replica_groups=mesh['ctx'=16,'tp'=8] {'tp'}, use_global_device_ids=true, to_apply=%region_27.28 | all-reduce | flops 2304 | bytes 18432 | tf_op jit(solution)/shard_map/psum | solution.py:310
  (494 shorter events, 335.6 us)
Async XLA Ops:
  7.2 44.8 %copy-start = (s32[16,2]{0,1:T(2,128)S(1)}, s32[16,2]{0,1:T(2,128)}, u32[]{:S(2)}) copy-start(s32[16,2]{0,1:T(2,128)} %param.22) | copy-start | bytes 388
  7.2 63.7 %all-gather.11.cloned.1.call-start = ((), (), s32[]{:S(2)}) async-start(), calls=%async_computation.9 | async-start | bytes 1114112 | tf_op jit(solution)/shard_map/all_gather | solution.py:122
  8.7 96.0 %all-gather.9.cloned.1.call-start = ((), (), s32[]{:S(2)}) async-start(), calls=%async_computation.8 | async-start | bytes 2359296 | tf_op jit(solution)/shard_map/all_gather | solution.py:130
  49.0 164.8 %all-gather.15.cloned.1.call-start = ((), (), s32[]{:S(2)}) async-start(), calls=%async_computation.11 | async-start | bytes 4456448 | tf_op jit(solution)/shard_map/all_gather | solution.py:147
  49.1 59.0 %copy-start.41 = (f32[128]{0:T(128)}, f32[128]{0:T(128)S(1)}, u32[]{:S(2)}) copy-start(f32[128]{0:T(128)S(1)} %convert_element_type.135) | copy-start | bytes 1540
  70.1 51.2 %copy-start.32 = (s32[1024]{0:T(1024)}, s32[1024]{0:T(1024)S(1)}, u32[]{:S(2)}) copy-start(s32[1024]{0:T(1024)S(1)} %get-tuple-element.1198) | copy-start | bytes 12292
  107.8 99.0 %copy-start.3 = (f32[1024,512]{0,1:T(8,128)}, f32[1024,512]{0,1:T(8,128)S(1)}, u32[]{:S(2)}) copy-start(f32[1024,512]{0,1:T(8,128)S(1)} %fusion.161) | copy-start | bytes 6291460
  112.1 158.1 %all-gather.13.cloned.1.call-start = ((), (), s32[]{:S(2)}) async-start(), calls=%async_computation.10 | async-start | bytes 4456448 | tf_op jit(solution)/shard_map/all_gather | solution.py:148
  121.3 36.5 %copy-start.34 = (s32[1024]{0:T(1024)}, s32[1024]{0:T(1024)S(1)}, u32[]{:S(2)}) copy-start(s32[1024]{0:T(1024)S(1)} %gather_fusion.3) | copy-start | bytes 12292
  157.9 23.6 %copy-start.40 = (bf16[256,64]{0,1:T(8,128)(2,1)S(1)}, bf16[256,64]{0,1:T(8,128)(2,1)}, u32[]{:S(2)}) copy-start(bf16[256,64]{0,1:T(8,128)(2,1)} %param.30) | copy-start | bytes 98308
  213.6 183.5 %reduce-scatter.10.cloned.1.call-start = ((), (), s32[]{:S(2)}) async-start(), calls=%async_computation.12 | async-start | bytes 2359296 | tf_op jit(solution)/shard_map/reduce_scatter | solution.py:202
  213.8 56.3 %copy-start.13 = (f32[4,256,1,2,128]{1,4,3,0,2:T(8,128)S(1)}, f32[4,256,1,2,128]{1,4,3,0,2:T(8,128)}, u32[]{:S(2)}) copy-start(f32[4,256,1,2,128]{1,4,3,0,2:T(8,128)} %custom-call.10) | copy-start | bytes 3145732
  325.5 71.5 %copy-start.5 = (bf16[128,1024]{1,0:T(8,128)(2,1)S(1)}, bf16[128,1024]{1,0:T(8,128)(2,1)}, u32[]{:S(2)}) copy-start(bf16[128,1024]{1,0:T(8,128)(2,1)} %param.21) | copy-start | bytes 786436
  327.7 106.1 %all-gather.19.cloned.1.call-start = ((), (), s32[]{:S(2)}) async-start(), calls=%async_computation.14 | async-start | bytes 1671168 | tf_op jit(solution)/shard_map/all_gather | solution.py:210
  328.4 161.0 %all-gather.17.cloned.1.call-start = ((), (), s32[]{:S(2)}) async-start(), calls=%async_computation.13 | async-start | bytes 2359296 | tf_op jit(solution)/shard_map/all_gather | solution.py:215
  400.0 143.6 %all-gather.21.cloned.1.call-start = ((), (), s32[]{:S(2)}) async-start(), calls=%async_computation.15 | async-start | bytes 2359296 | tf_op jit(solution)/shard_map/all_gather | solution.py:228
  400.8 235.3 %all-gather.23.cloned.1.call-start = ((), (), s32[]{:S(2)}) async-start(), calls=%async_computation.16 | async-start | bytes 2359296 | tf_op jit(solution)/shard_map/all_gather | solution.py:240
  424.7 118.9 %copy-start.24 = (bf16[384,1024]{0,1:T(8,128)(2,1)}, bf16[384,1024]{0,1:T(8,128)(2,1)S(1)}, u32[]{:S(2)}) copy-start(bf16[384,1024]{0,1:T(8,128)(2,1)S(1)} %all_gather.53) | copy-start | bytes 2359300
  582.4 56.8 %copy-start.47 = (f32[128]{0:T(128)}, f32[128]{0:T(128)S(1)}, u32[]{:S(2)}) copy-start(f32[128]{0:T(128)S(1)} %multiply_multiply_fusion.4) | copy-start | bytes 1540
  583.3 313.0 %reduce-scatter.14.cloned.1.call-start = ((), (), s32[]{:S(2)}) async-start(), calls=%async_computation.18 | async-start | bytes 4456448 | tf_op jit(solution)/shard_map/reduce_scatter | solution.py:292
  825.4 137.1 %reduce-scatter.12.cloned.1.call-start = ((), (), s32[]{:S(2)}) async-start(), calls=%async_computation.17 | async-start | bytes 4456448 | tf_op jit(solution)/shard_map/reduce_scatter | solution.py:289
  826.1 205.8 %reduce-scatter.18.cloned.1.call-start = ((), (), s32[]{:S(2)}) async-start(), calls=%async_computation.20 | async-start | bytes 2506752
  840.9 135.6 %all-to-all-start = ((bf16[8,128,1024]{2,1,0:T(8,128)(2,1)}), bf16[8,128,1024]{2,1,0:T(8,128)(2,1)}, u32[]{:S(2)}, u32[]{:S(2)}) async-start(bf16[8,128,1024]{2,1,0:T(8,128)(2,1)} %bitcast.391), calls=%async_computation.1 | async-start | bytes 4194304 | tf_op jit(solution)/shard_map/all_to_all | solution.py:20
  845.3 252.4 %reduce-scatter.16.cloned.1.call-start = ((), (), s32[]{:S(2)}) async-start(), calls=%async_computation.19 | async-start | bytes 1671168
  854.4 111.1 %copy-start.15 = (f32[1024,1,64]{0,2,1:T(8,128)S(1)}, f32[1024,1,64]{0,2,1:T(8,128)}, u32[]{:S(2)}) copy-start(f32[1024,1,64]{0,2,1:T(8,128)} %get-tuple-element.690) | copy-start | bytes 786436
  897.4 69.9 %copy-start.42 = (f32[128]{0:T(128)S(1)}, f32[128]{0:T(128)}, u32[]{:S(2)}) copy-start(f32[128]{0:T(128)} %copy-done.41) | copy-start | bytes 1540
  976.5 62.4 %all-to-all-start.2 = ((bf16[8,128,1024]{2,1,0:T(8,128)(2,1)}), bf16[8,128,1024]{2,1,0:T(8,128)(2,1)S(1)}, u32[]{:S(2)}, u32[]{:S(2)}) async-start(bf16[8,128,1024]{2,1,0:T(8,128)(2,1)} %bitcast.392), calls=%async_computation.5 | async-start | bytes 4194304 | tf_op jit(solution)/shard_map/all_to_all | solution.py:20
  1035.5 59.8 %copy-start.51 = (f32[128]{0:T(128)S(1)}, f32[128]{0:T(128)}, u32[]{:S(2)}) copy-start(f32[128]{0:T(128)} %copy-done.50) | copy-start | bytes 1540
  1035.5 59.8 %copy-start.9 = (f32[128,1024]{1,0:T(8,128)S(1)}, f32[128,1024]{1,0:T(8,128)}, u32[]{:S(2)}) copy-start(f32[128,1024]{1,0:T(8,128)} %copy-done.8) | copy-start | bytes 1572868
  1035.5 59.9 %copy-start.11 = (bf16[128,1024]{1,0:T(8,128)(2,1)S(1)}, bf16[128,1024]{1,0:T(8,128)(2,1)}, u32[]{:S(2)}) copy-start(bf16[128,1024]{1,0:T(8,128)(2,1)} %reduce-scatter.10.cloned.1.call-done) | copy-start | bytes 786436
  1035.5 59.9 %copy-start.17 = (bf16[128,1024]{1,0:T(8,128)(2,1)S(1)}, bf16[128,1024]{1,0:T(8,128)(2,1)}, u32[]{:S(2)}) copy-start(bf16[128,1024]{1,0:T(8,128)(2,1)} %param.35) | copy-start | bytes 786436
  1035.5 59.9 %copy-start.48 = (f32[128]{0:T(128)S(1)}, f32[128]{0:T(128)}, u32[]{:S(2)}) copy-start(f32[128]{0:T(128)} %copy-done.47) | copy-start | bytes 1540
  (45 other events, 111.5 us)
Sparse Core Ops, SparseCore 0:
  10.3 36.2 all-gather.10
  49.5 55.1 all-gather.8
  112.2 36.1 all-gather.14
  213.7 33.6 all-gather.12
  327.8 69.2 reduce-scatter.9
  399.2 34.5 all-gather.18
  436.7 52.6 all-gather.16
  491.8 51.7 all-gather.20
  583.4 52.5 all-gather.22
  825.5 70.7 reduce-scatter.13
  898.7 63.6 reduce-scatter.11
  964.7 67.1 reduce-scatter.17
  1034.3 61.0 reduce-scatter.15
